TPU v7x, 32 devices: a whole 2x2x4 slice. The times are simulated.
32 devices in a mesh: groups: 2 (over x), slab: 16 (over z, y, core).
Axes of the slice: x: 2, y: 2, z: 4, core: 2. Of those that a mesh axis runs over, the one named last changes fastest.
Arguments:
- latent: bfloat16 [64, 32, 2048], P(None, ('groups', 'slab')), parts along dimension 1, may hold values from -6 to 6
- conv1_weight: bfloat16 [27, 64, 64], replicated, may hold values from -0.15625 to 0.15625
- conv2_weight: bfloat16 [27, 64, 64], replicated, may hold values from -0.15625 to 0.15625
- head: bfloat16 [64], replicated, may hold values from -2 to 2
- p_prev: float32 [32, 16, 64, 128], P(('groups', 'slab')), parts along dimension 0, may hold values from -6 to 6
- p_cur: float32 [32, 16, 64, 128], P(('groups', 'slab')), parts along dimension 0, may hold values from -6 to 6
- adjoint: bfloat16 [4, 32, 16, 64, 128], P(None, ('groups', 'slab')), parts along dimension 1, may hold values from -6 to 6
- wavelet: float32 [16, 4], P('groups'), parts along dimension 0, may hold values from -12 to 12
- sources: int32 [16, 3], P('groups'), parts along dimension 0, may hold values from 0 to 127, as said below
- receivers: int32 [16, 3, 128], P('groups'), parts along dimension 0, may hold values from 0 to 127, as said below
Outputs:
- pressure_final: float32 [32, 16, 64, 128], P(('groups', 'slab')), parts along dimension 0
- traces: float32 [16, 4, 128], P('groups'), parts along dimension 0
- gradient: float32 [32, 2048], P(('groups', 'slab')), parts along dimension 0
There are 2 independent parts, one for each index of `groups`. A program takes and returns all parts, laid end to end along the dimension named above; an argument that names none is the same for every part. Nothing has to cross between parts.
Inputs may be any that keep to these rules, and one draw needn't show every extreme that they name: sources[s] is the source cell (depth, row, column) of shot s on the fine grid: depth below 32, row below 64, column below 128. receivers[s, :, k] is the cell (depth, row, column) of receiver k of shot s on the fine grid: depth below 32, row below 64, column below 128.
All inputs are finite; a program needn't handle non-finite values.
Results may differ from a plain program's by a relative error of at most 0.006.
Values may be sent and summed in bfloat16 or wider, within the bound.
A program may use at most 64 MiB of HBM per device.

v0:
```python
import jax
import jax.numpy as jnp
from jax import lax
from jax.sharding import PartitionSpec as P

CY = 32
CX = 64
SHOTS = 8
STEPS = 4
stencil_weights = (-205.0 / 72.0, 8.0 / 5.0, -1.0 / 5.0, 8.0 / 315.0, -1.0 / 560.0)
lowest_speed = 1.5
speed_range = 3.0
courant = 0.088
leak_slope = 0.2


def extended_2(block, sides, width):
    for axis, dim in sides:
        count = lax.axis_size(axis)
        forward = [(i, i + 1) for i in range(count - 1)]
        backward = [(target, source) for source, target in forward]
        low = lax.ppermute(
            lax.slice_in_dim(block, block.shape[dim] - width, None, axis=dim), axis, forward
        )
        high = lax.ppermute(lax.slice_in_dim(block, 0, width, axis=dim), axis, backward)
        block = jnp.concatenate([low, block, high], axis=dim)
    return block


def from_partner(value, axis, apart):
    mask = 2**apart
    pairs = [(source, source ^ mask) for source in range(lax.axis_size(axis))]
    return lax.ppermute(value, axis, pairs)


def for_sending(shard):
    return jax.tree.map(lambda a: a.astype(jnp.bfloat16) if a.dtype == jnp.float32 else a, shard)


def from_behind(value, axis, steps):
    count = lax.axis_size(axis)
    leading, last = (max(0, -steps), min(count, count - steps))
    return lax.ppermute(value, axis, [(source, source + steps) for source in range(leading, last)])


def conv_taps(extended_in, weight):
    planes = extended_in.shape[1] - 2
    cell_count = extended_in.shape[2]
    extended = jnp.pad(extended_in, ((0, 0), (0, 0), (CX + 1, CX + 1)))
    columns = jnp.arange(cell_count) % CX
    accumulated = jnp.zeros((weight.shape[1], planes, cell_count), jnp.float32)
    tap_index = 0
    for depth_off in range(3):
        for row_off in (-1, 0, 1):
            for col_off in (-1, 0, 1):
                begin_at = CX + 1 + row_off * CX + col_off
                piece = extended[
                    :, depth_off : depth_off + planes, begin_at : begin_at + cell_count
                ]
                column_valid = ((columns + col_off >= 0) & (columns + col_off < CX)).astype(
                    extended.dtype
                )
                accumulated = accumulated + jnp.einsum(
                    "oi,izn->ozn",
                    weight[tap_index],
                    piece * column_valid,
                    preferred_element_type=jnp.float32,
                )
                tap_index += 1
    return accumulated


def double_axis(values, axis):
    length = values.shape[axis]
    lower_side = jnp.concatenate(
        [
            lax.slice_in_dim(values, 0, 1, axis=axis),
            lax.slice_in_dim(values, 0, length - 1, axis=axis),
        ],
        axis=axis,
    )
    upper_side = jnp.concatenate(
        [
            lax.slice_in_dim(values, 1, length, axis=axis),
            lax.slice_in_dim(values, length - 1, length, axis=axis),
        ],
        axis=axis,
    )
    even_part = 0.75 * values + 0.25 * lower_side
    odd_part = 0.75 * values + 0.25 * upper_side
    new_shape = list(values.shape)
    new_shape[axis] = 2 * length
    return jnp.stack([even_part, odd_part], axis=axis + 1).reshape(new_shape)


def double_depth(rimmed):
    inner_planes = rimmed.shape[0] - 2
    middle = rimmed[1:-1]
    even_part = 0.75 * middle + 0.25 * rimmed[:-2]
    odd_part = 0.75 * middle + 0.25 * rimmed[2:]
    return jnp.stack([even_part, odd_part], axis=1).reshape((2 * inner_planes,) + rimmed.shape[1:])


def upsample_slab(rimmed):
    deeper = double_depth(rimmed).reshape(2 * (rimmed.shape[0] - 2), CY, CX)
    return double_axis(double_axis(deeper, 1), 2)


def stencil(extended):
    depth_total = extended.shape[0] - 8
    row_total = extended.shape[1]
    col_total = extended.shape[2]
    padded = jnp.pad(extended, ((0, 0), (4, 4), (4, 4)))

    def window(depth_at, row_at, col_at):
        return padded[
            depth_at : depth_at + depth_total,
            row_at : row_at + row_total,
            col_at : col_at + col_total,
        ]

    accumulated = 3.0 * stencil_weights[0] * window(4, 4, 4)
    for reach in range(1, 5):
        near_sum = window(4 - reach, 4, 4) + window(4 + reach, 4, 4)
        near_sum = near_sum + window(4, 4 - reach, 4) + window(4, 4 + reach, 4)
        near_sum = near_sum + window(4, 4, 4 - reach) + window(4, 4, 4 + reach)
        accumulated = accumulated + stencil_weights[reach] * near_sum
    return accumulated


def body(
    latent, conv1_weight, conv2_weight, head, p_prev, p_cur, adjoint, wavelet, sources, receivers
):
    position = lax.axis_index("slab")
    devices = lax.axis_size("slab")
    my_shot = position % SHOTS
    slab_index = position // SHOTS
    slab_total = devices // SHOTS
    group_bits = SHOTS.bit_length() - 1
    latent_wide = extended_2(latent, (("slab", 1),), 1)
    hidden = jax.nn.leaky_relu(conv_taps(latent_wide, conv1_weight), leak_slope).astype(
        jnp.bfloat16
    )
    hidden_wide = extended_2(hidden, (("slab", 1),), 1)
    second = jax.nn.leaky_relu(conv_taps(hidden_wide, conv2_weight), leak_slope)
    logits = jnp.einsum(
        "c,czn->zn", head.astype(jnp.float32), second, precision=lax.Precision.HIGHEST
    )
    velocity = (lowest_speed + speed_range * jax.nn.sigmoid(logits)).astype(jnp.bfloat16)
    planes = velocity.shape[0]
    slab_planes = planes * SHOTS
    rimmed = extended_2(velocity, (("slab", 0),), 1)
    rimmed = jnp.concatenate(
        [
            jnp.where(position == 0, velocity, rimmed[:1]),
            rimmed[1:-1],
            jnp.where(position == devices - 1, velocity, rimmed[-1:]),
        ],
        axis=0,
    )
    tile_doubled = double_depth(rimmed.astype(jnp.float32))
    bit_order = list(range(group_bits))
    blocks = tile_doubled[None]
    for bit_index in bit_order:
        partner = from_partner(blocks, "slab", bit_index)
        upper_bit = my_shot // (1 << bit_index) % 2 == 1
        blocks = jnp.where(
            upper_bit,
            jnp.concatenate([partner, blocks], axis=0),
            jnp.concatenate([blocks, partner], axis=0),
        )
    placed = []
    for shot_number in range(SHOTS):
        list_index = 0
        for section_number in range(group_bits):
            list_index = list_index + (
                (shot_number >> bit_order[section_number] & 1) << section_number
            )
        placed.append(blocks[list_index])
    deeper = jnp.concatenate(placed, axis=0).reshape(2 * slab_planes, CY, CX)
    fine_speed = double_axis(double_axis(deeper, 1), 2)
    courant_sq = (courant * fine_speed) ** 2
    previous = p_prev[0]
    current = p_cur[0]
    fine_planes = current.shape[0]
    offset = slab_index * fine_planes
    source = lax.dynamic_index_in_dim(sources, my_shot, 0, keepdims=False)
    station = lax.dynamic_index_in_dim(receivers, my_shot, 0, keepdims=False)
    pulses = lax.dynamic_index_in_dim(wavelet, my_shot, 0, keepdims=False)
    source_depth = source[0] - offset
    source_inside = (source_depth >= 0) & (source_depth < fine_planes)
    source_depth = jnp.clip(source_depth, 0, fine_planes - 1)
    station_depth = station[0] - offset
    station_inside = (station_depth >= 0) & (station_depth < fine_planes)
    station_depth = jnp.clip(station_depth, 0, fine_planes - 1)
    correlation = jnp.zeros(current.shape, jnp.float32)
    samples_list = []
    for step_index in range(STEPS):
        rim_below = from_behind(for_sending(current[-4:]), "slab", SHOTS)
        rim_above = from_behind(for_sending(current[:4]), "slab", -SHOTS)
        laplace_term = stencil(jnp.concatenate([rim_below, current, rim_above], axis=0))
        correlation = correlation + adjoint[step_index, 0].astype(jnp.float32) * laplace_term
        advanced = 2.0 * current - previous + courant_sq * laplace_term
        advanced = advanced.at[source_depth, source[1], source[2]].add(
            jnp.where(source_inside, pulses[step_index], 0.0)
        )
        samples_list.append(
            jnp.where(station_inside, advanced[station_depth, station[1], station[2]], 0.0)
        )
        previous, current = (current, advanced)
    record = jnp.stack(samples_list)
    own_traces = jnp.where((jnp.arange(SHOTS) == my_shot)[:, None, None], record[None], 0.0)
    traces = lax.psum(own_traces, "slab")
    fine_gradient = 2.0 * courant * courant * fine_speed * correlation
    shape_holder = jnp.zeros((slab_planes + 2, velocity.shape[1]), jnp.float32)
    unused, pullback = jax.vjp(upsample_slab, shape_holder)
    grad_rim = pullback(fine_gradient)[0]
    first_slab = slab_index == 0
    last_slab = slab_index == slab_total - 1
    folded = jnp.concatenate(
        [
            jnp.where(first_slab, 0.0, grad_rim[:1]),
            grad_rim[1:2] + jnp.where(first_slab, grad_rim[:1], 0.0),
            grad_rim[2:-2],
            grad_rim[-2:-1] + jnp.where(last_slab, grad_rim[-1:], 0.0),
            jnp.where(last_slab, 0.0, grad_rim[-1:]),
        ],
        axis=0,
    )
    from_lower = from_behind(folded[-1:], "slab", SHOTS)
    from_upper = from_behind(folded[:1], "slab", -SHOTS)
    inner = folded[1:-1]
    inner = jnp.concatenate([inner[:1] + from_lower, inner[1:-1], inner[-1:] + from_upper], axis=0)
    blocks = inner.reshape(SHOTS, planes, inner.shape[1])
    for bit_index in reversed(range(group_bits)):
        halfway = blocks.shape[0] // 2
        upper_bit = my_shot // (1 << bit_index) % 2 == 1
        retained = jnp.where(upper_bit, blocks[halfway:], blocks[:halfway])
        outgoing = jnp.where(upper_bit, blocks[:halfway], blocks[halfway:])
        blocks = retained + from_partner(outgoing, "slab", bit_index)
    gradient = blocks[0]
    return (current[None], traces, gradient)


def solution(mesh):
    in_specs = (
        P(None, ("groups", "slab"), None),
        P(),
        P(),
        P(),
        P(("groups", "slab"), None, None, None),
        P(("groups", "slab"), None, None, None),
        P(None, ("groups", "slab"), None, None, None),
        P("groups", None),
        P("groups", None),
        P("groups", None, None),
    )
    out_specs = (
        P(("groups", "slab"), None, None, None),
        P("groups", None, None),
        P(("groups", "slab"), None),
    )
    return jax.shard_map(body, mesh=mesh, in_specs=in_specs, out_specs=out_specs, check_vma=False)
```

profile of v0, /device:TPU:0, one launch (start us, length us, event | category | flops | bytes accessed | tf_op | source)
XLA Modules:
  0.0 228.8 jit_solution(11264955654170186735)
XLA Ops:
  0.7 1.4 collective-permute-start.1
  2.1 3.1 %collective-permute-start = (bf16[64,1,2048]{2,0,1:T(8,128)(2,1)}, bf16[64,1,2048]{2,0,1:T(8,128)(2,1)S(1)}, u32[]{:S(2)}, u32[]{:S(2)}) collective-permute-start(bf16[64,1,2048]{2,0,1:T(8,128)(2,1)} %param.18), channel_id=1, source_target_pairs={{0,1},{1,2},{2,3},{3,4},{4,5},{5,6},{6,7},{7,8},{8,9},{9,10},{10,1... | collective-permute-start | bytes 786440 | tf_op jit(solution)/shard_map/ppermute | solution.py:22
  5.2 1.1 convert.20
  6.5 1.3 fusion.32
  15.2 1.3 collective-permute-start.3
  16.5 9.2 %collective-permute-start.2 = (bf16[64,1,2048]{2,0,1:T(8,128)(2,1)S(1)}, bf16[64,1,2048]{2,0,1:T(8,128)(2,1)S(1)}, u32[]{:S(2)}, u32[]{:S(2)}) collective-permute-start(bf16[64,1,2048]{2,0,1:T(8,128)(2,1)S(1)} %bitcast.577), channel_id=1, source_target_pairs={{0,1},{1,2},{2,3},{3,4},{4,5},{5,6},{6,7},{7,8},{8,9},{9,10},{10,1... | collective-permute-start | bytes 786440 | tf_op jit(solution)/shard_map/ppermute | solution.py:22
  25.7 5.7 %collective-permute-start.9 = (bf16[4,64,128]{2,1,0:T(8,128)(2,1)S(1)}, bf16[4,64,128]{2,1,0:T(8,128)(2,1)S(1)}, u32[]{:S(2)}, u32[]{:S(2)}) collective-permute-start(bf16[4,64,128]{2,1,0:T(8,128)(2,1)S(1)} %get-tuple-element.81), channel_id=1, source_target_pairs={{0,8},{1,9},{2,10},{3,11},{4,12},{5,13},{6,14},{7,15},{16,24},{17,... | collective-permute-start | bytes 196616 | tf_op jit(solution)/shard_map/ppermute | solution.py:43
  31.4 1.3 collective-permute-start.10
  41.6 1.3 collective-permute-start.5
  42.9 3.6 %collective-permute-start.4 = (bf16[1,2048]{1,0:T(2,128)(2,1)S(1)}, bf16[1,2048]{1,0:T(2,128)(2,1)S(1)}, u32[]{:S(2)}, u32[]{:S(2)}) collective-permute-start(bf16[1,2048]{1,0:T(2,128)(2,1)S(1)} %convert_element_type.266), channel_id=1, source_target_pairs={{0,1},{1,2},{2,3},{3,4},{4,5},{5,6},{6,7},{7,8},{8,9},{9,10},{10,1... | collective-permute-start | bytes 12296 | tf_op jit(solution)/shard_map/ppermute | solution.py:22
  47.4 1.8 collective-permute-start.6
  54.2 2.4 %collective-permute-start.7 = (f32[2,2,2048]{2,1,0:T(2,128)S(1)}, f32[2,2,2048]{2,1,0:T(2,128)S(1)}, u32[]{:S(2)}, u32[]{:S(2)}) collective-permute-start(f32[2,2,2048]{2,1,0:T(2,128)S(1)} %maximum_select_fusion.2), channel_id=1, source_target_pairs={{0,2},{1,3},{2,0},{3,1},{4,6},{5,7},{6,4},{7,5},{8,10},{9,11},{10,... | collective-permute-start | bytes 98312 | tf_op jit(solution)/shard_map/ppermute | solution.py:33
  60.1 2.2 collective-permute-start.8
  62.8 1.7 collective-permute-done.8
  66.9 1.1 slice_bitcast_fusion.1
  69.2 1.3 copy.54
  71.1 1.1 copy.55
  72.2 1.7 fusion.155
  73.9 1.2 fusion.33
  75.1 1.9 copy.58
  77.0 1.6 copy.59
  78.6 4.4 %fusion.164 = (f32[16,64,128]{2,1,0:T(8,128)S(1)}, f32[16,64,128]{2,1,0:T(8,128)}) fusion(f32[1,16,64,128]{3,2,1,0:T(8,128)} %param.22, f32[16,64,128]{2,1,0:T(8,128)S(1)} %copy.59, f32[1,16,64,128]{3,2,1,0:T(8,128)S(1)} %copy-done.2, f32[24,72,136]{2,1,0:T(8,128)S(1)} %select_maximum_fusion.6, f32[4,64,128]{2,1,0:T(8,128)} %copy-done.11, ...), kind=kLoop, calls=%fused_computation.321 | loop fusion | flops 5373952 | bytes 11796480 | tf_op jit(solution)/shard_map/add | solution.py:203
  85.7 5.2 %collective-permute-start.11 = (bf16[4,64,128]{2,1,0:T(8,128)(2,1)S(1)}, bf16[4,64,128]{2,1,0:T(8,128)(2,1)S(1)}, u32[]{:S(2)}, u32[]{:S(2)}) collective-permute-start(bf16[4,64,128]{2,1,0:T(8,128)(2,1)S(1)} %get-tuple-element.79), channel_id=1, source_target_pairs={{0,8},{1,9},{2,10},{3,11},{4,12},{5,13},{6,14},{7,15},{16,24},{17,... | collective-permute-start | bytes 196616 | tf_op jit(solution)/shard_map/ppermute | solution.py:43
  90.8 1.3 collective-permute-start.12
  92.7 5.2 %collective-permute-done.12 = bf16[4,64,128]{2,1,0:T(8,128)(2,1)S(1)} collective-permute-done((bf16[4,64,128]{2,1,0:T(8,128)(2,1)S(1)}, bf16[4,64,128]{2,1,0:T(8,128)(2,1)S(1)}, u32[]{:S(2)}, u32[]{:S(2)}) %collective-permute-start.12) | collective-permute-done | bytes 65568 | tf_op jit(solution)/shard_map/ppermute | solution.py:43
  99.1 4.2 %multiply_add_fusion.2 = (f32[16,64,128]{2,1,0:T(8,128)S(1)}, f32[16,64,128]{2,1,0:T(8,128)}) fusion(f32[16,64,128]{2,1,0:T(8,128)} %copy-done.3, f32[16,64,128]{2,1,0:T(8,128)S(1)} %scatter-add.14, f32[1,16,64,128]{3,2,1,0:T(8,128)S(1)} %copy-done.2, f32[24,72,136]{2,1,0:T(8,128)S(1)} %select_maximum_fusion.4, f32[4,64,128]{2,1,0:T(8,128)} %copy-done.13, ...), kind=kLoop, calls=%fused_computation.326 | loop fusion | flops 5373952 | bytes 11272192 | tf_op jit(solution)/shard_map/add | solution.py:203
  106.1 1.6 collective-permute-start.13
  107.7 1.5 collective-permute-start.14
  110.0 1.5 gather_fusion
  111.5 3.3 %collective-permute-done.14 = bf16[4,64,128]{2,1,0:T(8,128)(2,1)S(1)} collective-permute-done((bf16[4,64,128]{2,1,0:T(8,128)(2,1)S(1)}, bf16[4,64,128]{2,1,0:T(8,128)(2,1)S(1)}, u32[]{:S(2)}, u32[]{:S(2)}) %collective-permute-start.14) | collective-permute-done | bytes 65568 | tf_op jit(solution)/shard_map/ppermute | solution.py:43
  116.0 4.2 %multiply_add_fusion.1 = (f32[16,64,128]{2,1,0:T(8,128)S(1)}, f32[16,64,128]{2,1,0:T(8,128)}) fusion(f32[16,64,128]{2,1,0:T(8,128)} %copy-done.3, f32[16,64,128]{2,1,0:T(8,128)S(1)} %scatter-add.14, f32[16,64,128]{2,1,0:T(8,128)S(1)} %scatter-add.15, f32[24,72,136]{2,1,0:T(8,128)S(1)} %select_maximum_fusion.2, f32[4,64,128]{2,1,0:T(8,128)} %copy-done.12, ...), kind=kLoop, calls=%fused_computation.325 | loop fusion | flops 5373952 | bytes 11272192 | tf_op jit(solution)/shard_map/add | solution.py:203
  123.0 2.2 collective-permute-start.15
  125.2 1.3 collective-permute-start.16
  127.2 2.0 copy.63
  129.2 2.4 %copy.64 = f32[16,64,128]{2,1,0:T(8,128)} copy(f32[16,64,128]{1,0,2:T(8,128)} %bitcast.569) | data formatting | bytes 1048576 | tf_op jit(solution)/shard_map/mul | solution.py:214
  131.6 1.5 gather_fusion.1
  133.1 1.5 gather_fusion.2
  136.0 3.4 %fusion.158 = (f32[16,64,128]{2,1,0:T(8,128)}, f32[16,64,128]{2,1,0:T(8,128)S(1)}) fusion(f32[16,64,128]{2,1,0:T(8,128)S(1)} %copy-done.10, f32[16,64,128]{2,1,0:T(8,128)S(1)} %copy-done.9, f32[16,64,128]{2,1,0:T(8,128)S(1)} %copy-done.8, f32[16,64,128]{2,1,0:T(8,128)S(1)} %copy-done.7, bf16[4,1,16,64,128]{4,3,2,1,0:T(8,128)(2,1)S(1)} %copy-done.14, ...), kind=kLoop, calls=%fused_computation.310 | loop fusion | flops 6422528 | bytes 13369344 | tf_op jit(solution)/shard_map/mul | solution.py:214
  142.2 1.5 gather_fusion.3
  143.7 1.5 copy.65
  148.5 5.4 %collective-permute-start.18 = (f32[1,2048]{1,0:T(1,128)S(1)}, f32[1,2048]{1,0:T(1,128)S(1)}, u32[]{:S(2)}, u32[]{:S(2)}) collective-permute-start(f32[1,2048]{1,0:T(1,128)S(1)} %get-tuple-element.91), channel_id=1, source_target_pairs={{0,8},{1,9},{2,10},{3,11},{4,12},{5,13},{6,14},{7,15},{16,24},{17,... | collective-permute-start | bytes 24584 | tf_op jit(solution)/shard_map/ppermute | solution.py:43
  153.9 1.3 collective-permute-start.17
  155.3 5.1 %collective-permute-done.17 = f32[1,2048]{1,0:T(1,128)S(1)} collective-permute-done((f32[1,2048]{1,0:T(1,128)S(1)}, f32[1,2048]{1,0:T(1,128)S(1)}, u32[]{:S(2)}, u32[]{:S(2)}) %collective-permute-start.17) | collective-permute-done | bytes 8224 | tf_op jit(solution)/shard_map/ppermute | solution.py:43
  160.5 2.1 collective-permute-start.19
  162.6 1.9 collective-permute-done.19
  164.5 1.8 collective-permute-start.20
  166.4 2.0 collective-permute-done.20
  168.4 59.7 %psum.7 = f32[8,4,128]{2,1,0:T(4,128)} all-reduce(f32[8,4,128]{2,1,0:T(4,128)S(1)} %broadcast_select_fusion.9), channel_id=1, replica_groups=mesh['groups'=2,'slab'=16] {'slab'}, use_global_device_ids=true, to_apply=%region_1.2 | all-reduce | flops 4096 | bytes 32768 | tf_op jit(solution)/shard_map/psum | solution.py:213
  (239 shorter events, 36.0 us)
Async XLA Ops:
  0.6 32.1 %copy-start = (f32[8,4]{0,1:T(4,128)S(1)}, f32[8,4]{0,1:T(4,128)}, u32[]{:S(2)}) copy-start(f32[8,4]{0,1:T(4,128)} %param.25) | copy-start | bytes 388
  0.6 7.1 %copy-start.17 = (bf16[27,64,64]{2,1,0:T(8,128)(2,1)S(1)}, bf16[27,64,64]{2,1,0:T(8,128)(2,1)}, u32[]{:S(2)}) copy-start(bf16[27,64,64]{2,1,0:T(8,128)(2,1)} %param.19) | copy-start | bytes 663556
  0.7 5.6 %collective-permute-start.1 = (bf16[64,1,2048]{2,0,1:T(8,128)(2,1)}, bf16[64,1,2048]{2,0,1:T(8,128)(2,1)S(1)}, u32[]{:S(2)}, u32[]{:S(2)}) collective-permute-start(bf16[64,1,2048]{2,0,1:T(8,128)(2,1)} %param.18), channel_id=1, source_target_pairs={{1,0},{2,1},{3,2},{4,3},{5,4},{6,5},{7,6},{8,7},{9,8},{10,9},{11,1... | collective-permute-start | bytes 786440 | tf_op jit(solution)/shard_map/ppermute | solution.py:25
  2.1 4.4 %collective-permute-start = (bf16[64,1,2048]{2,0,1:T(8,128)(2,1)}, bf16[64,1,2048]{2,0,1:T(8,128)(2,1)S(1)}, u32[]{:S(2)}, u32[]{:S(2)}) collective-permute-start(bf16[64,1,2048]{2,0,1:T(8,128)(2,1)} %param.18), channel_id=1, source_target_pairs={{0,1},{1,2},{2,3},{3,4},{4,5},{5,6},{6,7},{7,8},{8,9},{9,10},{10,1... | collective-permute-start | bytes 786440 | tf_op jit(solution)/shard_map/ppermute | solution.py:22
  11.8 1.0 copy-start.15
  14.9 19.0 %copy-start.16 = (bf16[27,64,64]{2,1,0:T(8,128)(2,1)S(1)}, bf16[27,64,64]{2,1,0:T(8,128)(2,1)}, u32[]{:S(2)}) copy-start(bf16[27,64,64]{2,1,0:T(8,128)(2,1)} %param.20) | copy-start | bytes 663556
  15.2 18.2 %collective-permute-start.3 = (bf16[64,1,2048]{2,0,1:T(8,128)(2,1)S(1)}, bf16[64,1,2048]{2,0,1:T(8,128)(2,1)S(1)}, u32[]{:S(2)}, u32[]{:S(2)}) collective-permute-start(bf16[64,1,2048]{2,0,1:T(8,128)(2,1)S(1)} %bitcast.576), channel_id=1, source_target_pairs={{1,0},{2,1},{3,2},{4,3},{5,4},{6,5},{7,6},{8,7},{9,8},{10,9},{11,1... | collective-permute-start | bytes 786440 | tf_op jit(solution)/shard_map/ppermute | solution.py:25
  16.5 16.9 %collective-permute-start.2 = (bf16[64,1,2048]{2,0,1:T(8,128)(2,1)S(1)}, bf16[64,1,2048]{2,0,1:T(8,128)(2,1)S(1)}, u32[]{:S(2)}, u32[]{:S(2)}) collective-permute-start(bf16[64,1,2048]{2,0,1:T(8,128)(2,1)S(1)} %bitcast.577), channel_id=1, source_target_pairs={{0,1},{1,2},{2,3},{3,4},{4,5},{5,6},{6,7},{7,8},{8,9},{9,10},{10,1... | collective-permute-start | bytes 786440 | tf_op jit(solution)/shard_map/ppermute | solution.py:22
  25.7 34.2 %collective-permute-start.9 = (bf16[4,64,128]{2,1,0:T(8,128)(2,1)S(1)}, bf16[4,64,128]{2,1,0:T(8,128)(2,1)S(1)}, u32[]{:S(2)}, u32[]{:S(2)}) collective-permute-start(bf16[4,64,128]{2,1,0:T(8,128)(2,1)S(1)} %get-tuple-element.81), channel_id=1, source_target_pairs={{0,8},{1,9},{2,10},{3,11},{4,12},{5,13},{6,14},{7,15},{16,24},{17,... | collective-permute-start | bytes 196616 | tf_op jit(solution)/shard_map/ppermute | solution.py:43
  31.4 28.6 %collective-permute-start.10 = (bf16[4,64,128]{2,1,0:T(8,128)(2,1)S(1)}, bf16[4,64,128]{2,1,0:T(8,128)(2,1)S(1)}, u32[]{:S(2)}, u32[]{:S(2)}) collective-permute-start(bf16[4,64,128]{2,1,0:T(8,128)(2,1)S(1)} %get-tuple-element.82), channel_id=1, source_target_pairs={{8,0},{9,1},{10,2},{11,3},{12,4},{13,5},{14,6},{15,7},{24,16},{25,... | collective-permute-start | bytes 196616 | tf_op jit(solution)/shard_map/ppermute | solution.py:43
  40.4 0.9 copy-start.19
  40.7 5.9 %copy-start.18 = (s32[8,3]{0,1:T(4,128)S(1)}, s32[8,3]{0,1:T(4,128)}, u32[]{:S(2)}) copy-start(s32[8,3]{0,1:T(4,128)} %param.26) | copy-start | bytes 292
  40.7 16.0 %copy-start.21 = (s32[3]{0:T(128)S(1)}, s32[3]{0:T(128)}, u32[]{:S(2)}) copy-start(s32[3]{0:T(128)} %constant.246.clone.1) | copy-start | bytes 40
  40.7 21.6 %copy-start.2 = (f32[1,16,64,128]{3,2,1,0:T(8,128)S(1)}, f32[1,16,64,128]{3,2,1,0:T(8,128)}, u32[]{:S(2)}) copy-start(f32[1,16,64,128]{3,2,1,0:T(8,128)} %param.23) | copy-start | bytes 1572868
  41.6 5.0 %collective-permute-start.5 = (bf16[1,2048]{1,0:T(2,128)(2,1)S(1)}, bf16[1,2048]{1,0:T(2,128)(2,1)S(1)}, u32[]{:S(2)}, u32[]{:S(2)}) collective-permute-start(bf16[1,2048]{1,0:T(2,128)(2,1)S(1)} %convert_element_type.266), channel_id=1, source_target_pairs={{1,0},{2,1},{3,2},{4,3},{5,4},{6,5},{7,6},{8,7},{9,8},{10,9},{11,1... | collective-permute-start | bytes 12296 | tf_op jit(solution)/shard_map/ppermute | solution.py:25
  42.9 4.3 %collective-permute-start.4 = (bf16[1,2048]{1,0:T(2,128)(2,1)S(1)}, bf16[1,2048]{1,0:T(2,128)(2,1)S(1)}, u32[]{:S(2)}, u32[]{:S(2)}) collective-permute-start(bf16[1,2048]{1,0:T(2,128)(2,1)S(1)} %convert_element_type.266), channel_id=1, source_target_pairs={{0,1},{1,2},{2,3},{3,4},{4,5},{5,6},{6,7},{7,8},{8,9},{9,10},{10,1... | collective-permute-start | bytes 12296 | tf_op jit(solution)/shard_map/ppermute | solution.py:22
  47.4 6.8 %collective-permute-start.6 = (f32[1,2,2048]{2,1,0:T(2,128)S(1)}, f32[1,2,2048]{2,1,0:T(2,128)S(1)}, u32[]{:S(2)}, u32[]{:S(2)}) collective-permute-start(f32[1,2,2048]{2,1,0:T(2,128)S(1)} %pad_maximum_fusion.12), channel_id=1, source_target_pairs={{0,1},{1,0},{2,3},{3,2},{4,5},{5,4},{6,7},{7,6},{8,9},{9,8},{10,11... | collective-permute-start | bytes 49160 | tf_op jit(solution)/shard_map/ppermute | solution.py:33
  54.2 5.8 %collective-permute-start.7 = (f32[2,2,2048]{2,1,0:T(2,128)S(1)}, f32[2,2,2048]{2,1,0:T(2,128)S(1)}, u32[]{:S(2)}, u32[]{:S(2)}) collective-permute-start(f32[2,2,2048]{2,1,0:T(2,128)S(1)} %maximum_select_fusion.2), channel_id=1, source_target_pairs={{0,2},{1,3},{2,0},{3,1},{4,6},{5,7},{6,4},{7,5},{8,10},{9,11},{10,... | collective-permute-start | bytes 98312 | tf_op jit(solution)/shard_map/ppermute | solution.py:33
  60.0 5.3 %copy-start.11 = (f32[4,64,128]{2,1,0:T(8,128)}, f32[4,64,128]{2,1,0:T(8,128)S(1)}, u32[]{:S(2)}) copy-start(f32[4,64,128]{2,1,0:T(8,128)S(1)} %convert_element_type.271) | copy-start | bytes 393220
  60.1 4.5 %collective-permute-start.8 = (f32[4,2,2048]{2,1,0:T(2,128)S(1)}, f32[4,2,2048]{2,1,0:T(2,128)S(1)}, u32[]{:S(2)}, u32[]{:S(2)}) collective-permute-start(f32[4,2,2048]{2,1,0:T(2,128)S(1)} %maximum_select_fusion.1), channel_id=1, source_target_pairs={{0,4},{1,5},{2,6},{3,7},{4,0},{5,1},{6,2},{7,3},{8,12},{9,13},{10,... | collective-permute-start | bytes 196616 | tf_op jit(solution)/shard_map/ppermute | solution.py:33
  78.6 4.4 %copy-start.3 = (f32[16,64,128]{2,1,0:T(8,128)}, f32[16,64,128]{2,1,0:T(8,128)S(1)}, u32[]{:S(2)}) copy-start(f32[16,64,128]{2,1,0:T(8,128)S(1)} %copy.59) | copy-start | bytes 1572868
  85.7 7.1 %collective-permute-start.11 = (bf16[4,64,128]{2,1,0:T(8,128)(2,1)S(1)}, bf16[4,64,128]{2,1,0:T(8,128)(2,1)S(1)}, u32[]{:S(2)}, u32[]{:S(2)}) collective-permute-start(bf16[4,64,128]{2,1,0:T(8,128)(2,1)S(1)} %get-tuple-element.79), channel_id=1, source_target_pairs={{0,8},{1,9},{2,10},{3,11},{4,12},{5,13},{6,14},{7,15},{16,24},{17,... | collective-permute-start | bytes 196616 | tf_op jit(solution)/shard_map/ppermute | solution.py:43
  90.8 7.1 %collective-permute-start.12 = (bf16[4,64,128]{2,1,0:T(8,128)(2,1)S(1)}, bf16[4,64,128]{2,1,0:T(8,128)(2,1)S(1)}, u32[]{:S(2)}, u32[]{:S(2)}) collective-permute-start(bf16[4,64,128]{2,1,0:T(8,128)(2,1)S(1)} %get-tuple-element.80), channel_id=1, source_target_pairs={{8,0},{9,1},{10,2},{11,3},{12,4},{13,5},{14,6},{15,7},{24,16},{25,... | collective-permute-start | bytes 196616 | tf_op jit(solution)/shard_map/ppermute | solution.py:43
  97.9 0.7 copy-start.13
  106.1 5.3 %collective-permute-start.13 = (bf16[4,64,128]{2,1,0:T(8,128)(2,1)S(1)}, bf16[4,64,128]{2,1,0:T(8,128)(2,1)S(1)}, u32[]{:S(2)}, u32[]{:S(2)}) collective-permute-start(bf16[4,64,128]{2,1,0:T(8,128)(2,1)S(1)} %get-tuple-element.77), channel_id=1, source_target_pairs={{0,8},{1,9},{2,10},{3,11},{4,12},{5,13},{6,14},{7,15},{16,24},{17,... | collective-permute-start | bytes 196616 | tf_op jit(solution)/shard_map/ppermute | solution.py:43
  107.7 7.1 %collective-permute-start.14 = (bf16[4,64,128]{2,1,0:T(8,128)(2,1)S(1)}, bf16[4,64,128]{2,1,0:T(8,128)(2,1)S(1)}, u32[]{:S(2)}, u32[]{:S(2)}) collective-permute-start(bf16[4,64,128]{2,1,0:T(8,128)(2,1)S(1)} %get-tuple-element.78), channel_id=1, source_target_pairs={{8,0},{9,1},{10,2},{11,3},{12,4},{13,5},{14,6},{15,7},{24,16},{25,... | collective-permute-start | bytes 196616 | tf_op jit(solution)/shard_map/ppermute | solution.py:43
  114.8 0.7 copy-start.12
  120.1 7.1 %copy-start.5 = (f32[16,64,64,2]{2,0,1,3:T(8,128)S(1)}, f32[16,64,64,2]{2,0,1,3:T(8,128)}, u32[]{:S(2)}) copy-start(f32[16,64,64,2]{2,0,1,3:T(8,128)} %get-tuple-element.63) | copy-start | bytes 1572868
  123.0 11.6 %collective-permute-start.15 = (bf16[4,64,128]{2,1,0:T(8,128)(2,1)S(1)}, bf16[4,64,128]{2,1,0:T(8,128)(2,1)S(1)}, u32[]{:S(2)}, u32[]{:S(2)}) collective-permute-start(bf16[4,64,128]{2,1,0:T(8,128)(2,1)S(1)} %get-tuple-element.75), channel_id=1, source_target_pairs={{0,8},{1,9},{2,10},{3,11},{4,12},{5,13},{6,14},{7,15},{16,24},{17,... | collective-permute-start | bytes 196616 | tf_op jit(solution)/shard_map/ppermute | solution.py:43
  125.2 9.4 %collective-permute-start.16 = (bf16[4,64,128]{2,1,0:T(8,128)(2,1)S(1)}, bf16[4,64,128]{2,1,0:T(8,128)(2,1)S(1)}, u32[]{:S(2)}, u32[]{:S(2)}) collective-permute-start(bf16[4,64,128]{2,1,0:T(8,128)(2,1)S(1)} %get-tuple-element.76), channel_id=1, source_target_pairs={{8,0},{9,1},{10,2},{11,3},{12,4},{13,5},{14,6},{15,7},{24,16},{25,... | collective-permute-start | bytes 196616 | tf_op jit(solution)/shard_map/ppermute | solution.py:43
  133.1 2.1 copy-start.7
  133.1 2.1 copy-start.8
  133.1 2.1 copy-start.9
  134.6 1.0 copy-start.10
  134.6 1.4 copy-start.14
  136.0 3.4 %copy-start.4 = (f32[16,64,128]{2,1,0:T(8,128)S(1)}, f32[16,64,128]{2,1,0:T(8,128)}, u32[]{:S(2)}) copy-start(f32[16,64,128]{2,1,0:T(8,128)} %copy-done.3) | copy-start | bytes 1572868
  142.2 3.1 %copy-start.6 = (f32[16,64,128]{2,1,0:T(8,128)}, f32[16,64,128]{2,1,0:T(8,128)S(1)}, u32[]{:S(2)}) copy-start(f32[16,64,128]{2,1,0:T(8,128)S(1)} %scatter-add.19) | copy-start | bytes 1572868
  146.1 0.7 copy-start.22
  147.1 0.7 copy-start.20
  147.4 81.3 %copy-start.1 = (f32[8,4]{0,1:T(4,128)S(1)}, f32[8,4]{0,1:T(4,128)}, u32[]{:S(2)}) copy-start(f32[8,4]{0,1:T(4,128)} %param.25) | copy-start | bytes 388
  148.5 6.8 %collective-permute-start.18 = (f32[1,2048]{1,0:T(1,128)S(1)}, f32[1,2048]{1,0:T(1,128)S(1)}, u32[]{:S(2)}, u32[]{:S(2)}) collective-permute-start(f32[1,2048]{1,0:T(1,128)S(1)} %get-tuple-element.91), channel_id=1, source_target_pairs={{0,8},{1,9},{2,10},{3,11},{4,12},{5,13},{6,14},{7,15},{16,24},{17,... | collective-permute-start | bytes 24584 | tf_op jit(solution)/shard_map/ppermute | solution.py:43
  153.9 6.4 %collective-permute-start.17 = (f32[1,2048]{1,0:T(1,128)S(1)}, f32[1,2048]{1,0:T(1,128)S(1)}, u32[]{:S(2)}, u32[]{:S(2)}) collective-permute-start(f32[1,2048]{1,0:T(1,128)S(1)} %get-tuple-element.92), channel_id=1, source_target_pairs={{8,0},{9,1},{10,2},{11,3},{12,4},{13,5},{14,6},{15,7},{24,16},{25,... | collective-permute-start | bytes 24584 | tf_op jit(solution)/shard_map/ppermute | solution.py:43
  160.5 4.0 %collective-permute-start.19 = (f32[4,1,2048]{2,0,1:T(4,128)S(1)}, f32[4,1,2048]{2,0,1:T(4,128)S(1)}, u32[]{:S(2)}, u32[]{:S(2)}) collective-permute-start(f32[4,1,2048]{2,0,1:T(4,128)S(1)} %select_bitcast_fusion), channel_id=1, source_target_pairs={{0,4},{1,5},{2,6},{3,7},{4,0},{5,1},{6,2},{7,3},{8,12},{9,13},{10,... | collective-permute-start | bytes 98312 | tf_op jit(solution)/shard_map/ppermute | solution.py:33
  164.5 3.8 %collective-permute-start.20 = (f32[2,1,2048]{2,0,1:T(2,128)S(1)}, f32[2,1,2048]{2,0,1:T(2,128)S(1)}, u32[]{:S(2)}, u32[]{:S(2)}) collective-permute-start(f32[2,1,2048]{2,0,1:T(2,128)S(1)} %broadcast_select_fusion.4), channel_id=1, source_target_pairs={{0,2},{1,3},{2,0},{3,1},{4,6},{5,7},{6,4},{7,5},{8,10},{9,11},{10,... | collective-permute-start | bytes 49160 | tf_op jit(solution)/shard_map/ppermute | solution.py:33
  168.3 59.8 %collective-permute-start.21 = (f32[1,1,2048]{2,0,1:T(1,128)S(1)}, f32[1,1,2048]{2,0,1:T(1,128)S(1)}, u32[]{:S(2)}, u32[]{:S(2)}) collective-permute-start(f32[1,1,2048]{2,0,1:T(1,128)S(1)} %broadcast_select_fusion.5), channel_id=1, source_target_pairs={{0,1},{1,0},{2,3},{3,2},{4,5},{5,4},{6,7},{7,6},{8,9},{9,8},{10,11... | collective-permute-start | bytes 24584 | tf_op jit(solution)/shard_map/ppermute | solution.py:33
where the time goes:
time: 230 us; the launch traced here: 229 us
  blocking collectives  59.7 us (26%)
  starting transfers between devices  56.9 us (25%)
  local copies, waits for them, and re-layouts  31.1 us (14%)
  other arithmetic  28.9 us (13%)
  waiting for transfers between devices  20.4 us (9%)
  between operations  16.9 us (7%)
  matrix products  14.7 us (6%)
    psum x1, blocking collectives, body(): traces = lax.psum(own_traces, 'slab')  59.7 us
    ppermute x10, starting transfers between devices, from_behind(): lax.ppermute(value, axis, [(source, source + steps) for source in range(l...  26.7 us
    ppermute x3, starting transfers between devices, extended_2(): lax.ppermute(lax.slice_in_dim(block, block.shape[dim] - width, None, axis...  15.9 us
    dot_general x54, matrix products, conv_taps(): jnp.einsum('oi,izn->ozn', weight[tap_index], piece * column_valid, prefer...  14.4 us
    ppermute x10, waiting for transfers between devices, from_behind(): lax.ppermute(value, axis, [(source, source + steps) for source in range(l...  14.1 us
    add x4, other arithmetic, body(): advanced = 2.0 * current - previous + courant_sq * laplace_term  12.9 us
    ppermute x6, starting transfers between devices, from_partner(): return lax.ppermute(value, axis, pairs)  10.4 us
    gather x4, local copies, waits for them, and re-layouts, body(): advanced[station_depth, station[1], station[2]]  5.93 us
  transfers between devices with their start and end apart: 22, of which 9 were waited for; matrix products, arithmetic and copies ran while one was open for 10% of the time, Pallas kernels for 0%

commit v1 on v0

--- a/solution.py
+++ b/solution.py
@@ -12,6 +12,15 @@
 speed_range = 3.0
 courant = 0.088
 leak_slope = 0.2
+
+
+def add_in_pairs(block, name):
+    size = lax.axis_size(name)
+    total, reach = (block, 1)
+    while reach < size:
+        total = total + lax.ppermute(total, name, [(i, i ^ reach) for i in range(size)])
+        reach = 2 * reach
+    return total
 
 
 def extended_2(block, sides, width):
@@ -210,7 +219,7 @@
         previous, current = (current, advanced)
     record = jnp.stack(samples_list)
     own_traces = jnp.where((jnp.arange(SHOTS) == my_shot)[:, None, None], record[None], 0.0)
-    traces = lax.psum(own_traces, "slab")
+    traces = add_in_pairs(own_traces, "slab")
     fine_gradient = 2.0 * courant * courant * fine_speed * correlation
     shape_holder = jnp.zeros((slab_planes + 2, velocity.shape[1]), jnp.float32)
     unused, pullback = jax.vjp(upsample_slab, shape_holder)

time: 230 us -> 175 us (0.76)
  blocking collectives: 59.7 us -> 0 us
  starting transfers between devices: 56.9 us -> 60.3 us
    psum x1 -> x0, blocking collectives: 59.7 us -> none  [body(): traces = lax.psum(own_traces, 'slab')]
    ppermute x0 -> x4, starting transfers between devices: none -> 3.77 us  [add_in_pairs(): lax.ppermute(total, name, [(i, i ^ reach) for i in range(size)])]
    ppermute x0 -> x4, waiting for transfers between devices: none -> 2.88 us  [add_in_pairs(): lax.ppermute(total, name, [(i, i ^ reach) for i in range(size)])]
  transfers between devices with their start and end apart: 22 -> 26, of which waited for: 9 -> 11; matrix products, arithmetic and copies ran while one was open for 10% -> 13% of each run, Pallas kernels for 0% -> 0%
where the time goes in v1:
time: 175 us; the launch traced here: 174 us
  starting transfers between devices  60.3 us (34%)
  local copies, waits for them, and re-layouts  31.1 us (18%)
  other arithmetic  29.7 us (17%)
  waiting for transfers between devices  21.4 us (12%)
  between operations  17.2 us (10%)
  matrix products  14.7 us (8%)
    ppermute x10, starting transfers between devices, from_behind(): lax.ppermute(value, axis, [(source, source + steps) for source in range(l...  26.7 us
    ppermute x3, starting transfers between devices, extended_2(): lax.ppermute(lax.slice_in_dim(block, block.shape[dim] - width, None, axis...  15.9 us
    dot_general x54, matrix products, conv_taps(): jnp.einsum('oi,izn->ozn', weight[tap_index], piece * column_valid, prefer...  14.4 us
    ppermute x10, waiting for transfers between devices, from_behind(): lax.ppermute(value, axis, [(source, source + steps) for source in range(l...  14 us
    add x4, other arithmetic, body(): advanced = 2.0 * current - previous + courant_sq * laplace_term  12.9 us
    ppermute x6, starting transfers between devices, from_partner(): return lax.ppermute(value, axis, pairs)  9.89 us
    gather x4, local copies, waits for them, and re-layouts, body(): advanced[station_depth, station[1], station[2]]  5.93 us
    mul x3, local copies, waits for them, and re-layouts, body(): fine_gradient = 2.0 * courant * courant * fine_speed * correlation  5.89 us
  transfers between devices with their start and end apart: 26, of which 11 were waited for; matrix products, arithmetic and copies ran while one was open for 13% of the time, Pallas kernels for 0%

profile of v1, /device:TPU:0, one launch (start us, length us, event | category | flops | bytes accessed | tf_op | source)
XLA Modules:
  0.0 174.3 jit_solution(10183999659742342518)
XLA Ops:
  0.7 1.4 collective-permute-start.1
  2.1 3.1 %collective-permute-start = (bf16[64,1,2048]{2,0,1:T(8,128)(2,1)}, bf16[64,1,2048]{2,0,1:T(8,128)(2,1)S(1)}, u32[]{:S(2)}, u32[]{:S(2)}) collective-permute-start(bf16[64,1,2048]{2,0,1:T(8,128)(2,1)} %param.18), channel_id=1, source_target_pairs={{0,1},{1,2},{2,3},{3,4},{4,5},{5,6},{6,7},{7,8},{8,9},{9,10},{10,1... | collective-permute-start | bytes 786440 | tf_op jit(solution)/shard_map/ppermute | solution.py:31
  5.2 1.1 convert.20
  6.5 1.3 fusion.32
  15.2 1.3 collective-permute-start.3
  16.5 9.2 %collective-permute-start.2 = (bf16[64,1,2048]{2,0,1:T(8,128)(2,1)S(1)}, bf16[64,1,2048]{2,0,1:T(8,128)(2,1)S(1)}, u32[]{:S(2)}, u32[]{:S(2)}) collective-permute-start(bf16[64,1,2048]{2,0,1:T(8,128)(2,1)S(1)} %bitcast.577), channel_id=1, source_target_pairs={{0,1},{1,2},{2,3},{3,4},{4,5},{5,6},{6,7},{7,8},{8,9},{9,10},{10,1... | collective-permute-start | bytes 786440 | tf_op jit(solution)/shard_map/ppermute | solution.py:31
  25.7 5.7 %collective-permute-start.9 = (bf16[4,64,128]{2,1,0:T(8,128)(2,1)S(1)}, bf16[4,64,128]{2,1,0:T(8,128)(2,1)S(1)}, u32[]{:S(2)}, u32[]{:S(2)}) collective-permute-start(bf16[4,64,128]{2,1,0:T(8,128)(2,1)S(1)} %get-tuple-element.81), channel_id=1, source_target_pairs={{0,8},{1,9},{2,10},{3,11},{4,12},{5,13},{6,14},{7,15},{16,24},{17,... | collective-permute-start | bytes 196616 | tf_op jit(solution)/shard_map/ppermute | solution.py:52
  31.4 1.3 collective-permute-start.10
  41.6 1.3 collective-permute-start.5
  42.9 3.6 %collective-permute-start.4 = (bf16[1,2048]{1,0:T(2,128)(2,1)S(1)}, bf16[1,2048]{1,0:T(2,128)(2,1)S(1)}, u32[]{:S(2)}, u32[]{:S(2)}) collective-permute-start(bf16[1,2048]{1,0:T(2,128)(2,1)S(1)} %convert_element_type.266), channel_id=1, source_target_pairs={{0,1},{1,2},{2,3},{3,4},{4,5},{5,6},{6,7},{7,8},{8,9},{9,10},{10,1... | collective-permute-start | bytes 12296 | tf_op jit(solution)/shard_map/ppermute | solution.py:31
  47.4 1.8 %collective-permute-start.6 = (f32[1,2,2048]{2,1,0:T(2,128)S(1)}, f32[1,2,2048]{2,1,0:T(2,128)S(1)}, u32[]{:S(2)}, u32[]{:S(2)}) collective-permute-start(f32[1,2,2048]{2,1,0:T(2,128)S(1)} %pad_maximum_fusion.12), channel_id=1, source_target_pairs={{0,1},{1,0},{2,3},{3,2},{4,5},{5,4},{6,7},{7,6},{8,9},{9,8},{10,11... | collective-permute-start | bytes 49160 | tf_op jit(solution)/shard_map/ppermute | solution.py:42
  54.2 2.4 %collective-permute-start.7 = (f32[2,2,2048]{2,1,0:T(2,128)S(1)}, f32[2,2,2048]{2,1,0:T(2,128)S(1)}, u32[]{:S(2)}, u32[]{:S(2)}) collective-permute-start(f32[2,2,2048]{2,1,0:T(2,128)S(1)} %maximum_select_fusion.2), channel_id=1, source_target_pairs={{0,2},{1,3},{2,0},{3,1},{4,6},{5,7},{6,4},{7,5},{8,10},{9,11},{10,... | collective-permute-start | bytes 98312 | tf_op jit(solution)/shard_map/ppermute | solution.py:42
  60.1 2.2 %collective-permute-start.8 = (f32[4,2,2048]{2,1,0:T(2,128)S(1)}, f32[4,2,2048]{2,1,0:T(2,128)S(1)}, u32[]{:S(2)}, u32[]{:S(2)}) collective-permute-start(f32[4,2,2048]{2,1,0:T(2,128)S(1)} %maximum_select_fusion.1), channel_id=1, source_target_pairs={{0,4},{1,5},{2,6},{3,7},{4,0},{5,1},{6,2},{7,3},{8,12},{9,13},{10,... | collective-permute-start | bytes 196616 | tf_op jit(solution)/shard_map/ppermute | solution.py:42
  62.8 1.8 %collective-permute-done.8 = f32[4,2,2048]{2,1,0:T(2,128)S(1)} collective-permute-done((f32[4,2,2048]{2,1,0:T(2,128)S(1)}, f32[4,2,2048]{2,1,0:T(2,128)S(1)}, u32[]{:S(2)}, u32[]{:S(2)}) %collective-permute-start.8) | collective-permute-done | bytes 65568 | tf_op jit(solution)/shard_map/ppermute | solution.py:42
  66.9 1.1 slice_bitcast_fusion.1
  69.3 1.3 copy.54
  72.2 1.7 fusion.155
  74.0 1.2 fusion.33
  75.1 1.9 %copy.58 = f32[16,64,64,2]{1,0,3,2:T(8,128)} copy(f32[16,64,64,2]{2,0,1,3:T(8,128)S(1)} %get-tuple-element.64) | data formatting | bytes 1048576 | tf_op jit(solution)/shard_map/integer_pow | solution.py:191
  77.0 1.6 copy.59
  78.7 4.3 %fusion.164 = (f32[16,64,128]{2,1,0:T(8,128)S(1)}, f32[16,64,128]{2,1,0:T(8,128)}) fusion(f32[1,16,64,128]{3,2,1,0:T(8,128)} %param.22, f32[16,64,128]{2,1,0:T(8,128)S(1)} %copy.59, f32[1,16,64,128]{3,2,1,0:T(8,128)S(1)} %copy-done.2, f32[24,72,136]{2,1,0:T(8,128)S(1)} %select_maximum_fusion.6, f32[4,64,128]{2,1,0:T(8,128)} %copy-done.11, ...), kind=kLoop, calls=%fused_computation.321 | loop fusion | flops 5373952 | bytes 11796480 | tf_op jit(solution)/shard_map/add | solution.py:212
  85.8 5.2 %collective-permute-start.11 = (bf16[4,64,128]{2,1,0:T(8,128)(2,1)S(1)}, bf16[4,64,128]{2,1,0:T(8,128)(2,1)S(1)}, u32[]{:S(2)}, u32[]{:S(2)}) collective-permute-start(bf16[4,64,128]{2,1,0:T(8,128)(2,1)S(1)} %get-tuple-element.79), channel_id=1, source_target_pairs={{0,8},{1,9},{2,10},{3,11},{4,12},{5,13},{6,14},{7,15},{16,24},{17,... | collective-permute-start | bytes 196616 | tf_op jit(solution)/shard_map/ppermute | solution.py:52
  91.0 1.3 collective-permute-start.12
  92.9 5.2 %collective-permute-done.12 = bf16[4,64,128]{2,1,0:T(8,128)(2,1)S(1)} collective-permute-done((bf16[4,64,128]{2,1,0:T(8,128)(2,1)S(1)}, bf16[4,64,128]{2,1,0:T(8,128)(2,1)S(1)}, u32[]{:S(2)}, u32[]{:S(2)}) %collective-permute-start.12) | collective-permute-done | bytes 65568 | tf_op jit(solution)/shard_map/ppermute | solution.py:52
  99.2 4.2 %multiply_add_fusion.2 = (f32[16,64,128]{2,1,0:T(8,128)S(1)}, f32[16,64,128]{2,1,0:T(8,128)}) fusion(f32[16,64,128]{2,1,0:T(8,128)} %copy-done.3, f32[16,64,128]{2,1,0:T(8,128)S(1)} %scatter-add.14, f32[1,16,64,128]{3,2,1,0:T(8,128)S(1)} %copy-done.2, f32[24,72,136]{2,1,0:T(8,128)S(1)} %select_maximum_fusion.4, f32[4,64,128]{2,1,0:T(8,128)} %copy-done.13, ...), kind=kLoop, calls=%fused_computation.326 | loop fusion | flops 5373952 | bytes 11272192 | tf_op jit(solution)/shard_map/add | solution.py:212
  106.3 1.6 collective-permute-start.13
  107.9 1.5 collective-permute-start.14
  110.2 1.5 gather_fusion
  111.7 3.3 %collective-permute-done.14 = bf16[4,64,128]{2,1,0:T(8,128)(2,1)S(1)} collective-permute-done((bf16[4,64,128]{2,1,0:T(8,128)(2,1)S(1)}, bf16[4,64,128]{2,1,0:T(8,128)(2,1)S(1)}, u32[]{:S(2)}, u32[]{:S(2)}) %collective-permute-start.14) | collective-permute-done | bytes 65568 | tf_op jit(solution)/shard_map/ppermute | solution.py:52
  116.2 4.2 %multiply_add_fusion.1 = (f32[16,64,128]{2,1,0:T(8,128)S(1)}, f32[16,64,128]{2,1,0:T(8,128)}) fusion(f32[16,64,128]{2,1,0:T(8,128)} %copy-done.3, f32[16,64,128]{2,1,0:T(8,128)S(1)} %scatter-add.14, f32[16,64,128]{2,1,0:T(8,128)S(1)} %scatter-add.15, f32[24,72,136]{2,1,0:T(8,128)S(1)} %select_maximum_fusion.2, f32[4,64,128]{2,1,0:T(8,128)} %copy-done.12, ...), kind=kLoop, calls=%fused_computation.325 | loop fusion | flops 5373952 | bytes 11272192 | tf_op jit(solution)/shard_map/add | solution.py:212
  123.2 2.2 %collective-permute-start.15 = (bf16[4,64,128]{2,1,0:T(8,128)(2,1)S(1)}, bf16[4,64,128]{2,1,0:T(8,128)(2,1)S(1)}, u32[]{:S(2)}, u32[]{:S(2)}) collective-permute-start(bf16[4,64,128]{2,1,0:T(8,128)(2,1)S(1)} %get-tuple-element.75), channel_id=1, source_target_pairs={{0,8},{1,9},{2,10},{3,11},{4,12},{5,13},{6,14},{7,15},{16,24},{17,... | collective-permute-start | bytes 196616 | tf_op jit(solution)/shard_map/ppermute | solution.py:52
  125.4 1.3 collective-permute-start.16
  127.4 1.9 %copy.63 = f32[16,64,64,2]{1,0,3,2:T(8,128)} copy(f32[16,64,64,2]{2,0,1,3:T(8,128)S(1)} %copy-done.5) | data formatting | bytes 1048576 | tf_op jit(solution)/shard_map/mul | solution.py:223
  129.3 2.4 %copy.64 = f32[16,64,128]{2,1,0:T(8,128)} copy(f32[16,64,128]{1,0,2:T(8,128)} %bitcast.569) | data formatting | bytes 1048576 | tf_op jit(solution)/shard_map/mul | solution.py:223
  131.7 1.5 gather_fusion.1
  133.2 1.5 gather_fusion.2
  136.1 3.3 %fusion.158 = (f32[16,64,128]{2,1,0:T(8,128)}, f32[16,64,128]{2,1,0:T(8,128)S(1)}) fusion(f32[16,64,128]{2,1,0:T(8,128)S(1)} %copy-done.10, f32[16,64,128]{2,1,0:T(8,128)S(1)} %copy-done.9, f32[16,64,128]{2,1,0:T(8,128)S(1)} %copy-done.8, f32[16,64,128]{2,1,0:T(8,128)S(1)} %copy-done.7, bf16[4,1,16,64,128]{4,3,2,1,0:T(8,128)(2,1)S(1)} %copy-done.14, ...), kind=kLoop, calls=%fused_computation.310 | loop fusion | flops 6422528 | bytes 13369344 | tf_op jit(solution)/shard_map/mul | solution.py:223
  142.4 1.5 gather_fusion.3
  143.9 1.5 copy.65
  148.7 5.4 %collective-permute-start.22 = (f32[1,2048]{1,0:T(1,128)S(1)}, f32[1,2048]{1,0:T(1,128)S(1)}, u32[]{:S(2)}, u32[]{:S(2)}) collective-permute-start(f32[1,2048]{1,0:T(1,128)S(1)} %get-tuple-element.91), channel_id=1, source_target_pairs={{0,8},{1,9},{2,10},{3,11},{4,12},{5,13},{6,14},{7,15},{16,24},{17,... | collective-permute-start | bytes 24584 | tf_op jit(solution)/shard_map/ppermute | solution.py:52
  154.1 1.3 collective-permute-start.21
  155.6 5.0 %collective-permute-done.21 = f32[1,2048]{1,0:T(1,128)S(1)} collective-permute-done((f32[1,2048]{1,0:T(1,128)S(1)}, f32[1,2048]{1,0:T(1,128)S(1)}, u32[]{:S(2)}, u32[]{:S(2)}) %collective-permute-start.21) | collective-permute-done | bytes 8224 | tf_op jit(solution)/shard_map/ppermute | solution.py:52
  160.7 1.8 %collective-permute-start.18 = (f32[8,4,128]{2,1,0:T(4,128)S(1)}, f32[8,4,128]{2,1,0:T(4,128)S(1)}, u32[]{:S(2)}, u32[]{:S(2)}) collective-permute-start(f32[8,4,128]{2,1,0:T(4,128)S(1)} %fusion.474), channel_id=1, source_target_pairs={{0,2},{1,3},{2,0},{3,1},{4,6},{5,7},{6,4},{7,5},{8,10},{9,11},{10,... | collective-permute-start | bytes 49160 | tf_op jit(solution)/shard_map/ppermute | solution.py:21
  162.5 1.9 %collective-permute-start.23 = (f32[4,1,2048]{2,0,1:T(4,128)S(1)}, f32[4,1,2048]{2,0,1:T(4,128)S(1)}, u32[]{:S(2)}, u32[]{:S(2)}) collective-permute-start(f32[4,1,2048]{2,0,1:T(4,128)S(1)} %select_bitcast_fusion), channel_id=1, source_target_pairs={{0,4},{1,5},{2,6},{3,7},{4,0},{5,1},{6,2},{7,3},{8,12},{9,13},{10,... | collective-permute-start | bytes 98312 | tf_op jit(solution)/shard_map/ppermute | solution.py:42
  164.7 2.0 %collective-permute-start.19 = (f32[8,4,128]{2,1,0:T(4,128)S(1)}, f32[8,4,128]{2,1,0:T(4,128)S(1)}, u32[]{:S(2)}, u32[]{:S(2)}) collective-permute-start(f32[8,4,128]{2,1,0:T(4,128)S(1)} %fusion.500), channel_id=1, source_target_pairs={{0,4},{1,5},{2,6},{3,7},{4,0},{5,1},{6,2},{7,3},{8,12},{9,13},{10,... | collective-permute-start | bytes 49160 | tf_op jit(solution)/shard_map/ppermute | solution.py:21
  166.7 1.6 collective-permute-start.24
  168.5 2.0 %collective-permute-done.24 = f32[2,1,2048]{2,0,1:T(2,128)S(1)} collective-permute-done((f32[2,1,2048]{2,0,1:T(2,128)S(1)}, f32[2,1,2048]{2,0,1:T(2,128)S(1)}, u32[]{:S(2)}, u32[]{:S(2)}) %collective-permute-start.24) | collective-permute-done | bytes 16416 | tf_op jit(solution)/shard_map/ppermute | solution.py:42
  170.6 2.5 %collective-permute-done.20 = f32[8,4,128]{2,1,0:T(4,128)S(1)} collective-permute-done((f32[8,4,128]{2,1,0:T(4,128)S(1)}, f32[8,4,128]{2,1,0:T(4,128)S(1)}, u32[]{:S(2)}, u32[]{:S(2)}) %collective-permute-start.20) | collective-permute-done | bytes 16416 | tf_op jit(solution)/shard_map/ppermute | solution.py:21
  (250 shorter events, 38.2 us)
Async XLA Ops:
  0.6 32.1 %copy-start = (f32[8,4]{0,1:T(4,128)S(1)}, f32[8,4]{0,1:T(4,128)}, u32[]{:S(2)}) copy-start(f32[8,4]{0,1:T(4,128)} %param.25) | copy-start | bytes 388
  0.6 7.1 %copy-start.17 = (bf16[27,64,64]{2,1,0:T(8,128)(2,1)S(1)}, bf16[27,64,64]{2,1,0:T(8,128)(2,1)}, u32[]{:S(2)}) copy-start(bf16[27,64,64]{2,1,0:T(8,128)(2,1)} %param.19) | copy-start | bytes 663556
  0.7 5.6 %collective-permute-start.1 = (bf16[64,1,2048]{2,0,1:T(8,128)(2,1)}, bf16[64,1,2048]{2,0,1:T(8,128)(2,1)S(1)}, u32[]{:S(2)}, u32[]{:S(2)}) collective-permute-start(bf16[64,1,2048]{2,0,1:T(8,128)(2,1)} %param.18), channel_id=1, source_target_pairs={{1,0},{2,1},{3,2},{4,3},{5,4},{6,5},{7,6},{8,7},{9,8},{10,9},{11,1... | collective-permute-start | bytes 786440 | tf_op jit(solution)/shard_map/ppermute | solution.py:34
  2.1 4.4 %collective-permute-start = (bf16[64,1,2048]{2,0,1:T(8,128)(2,1)}, bf16[64,1,2048]{2,0,1:T(8,128)(2,1)S(1)}, u32[]{:S(2)}, u32[]{:S(2)}) collective-permute-start(bf16[64,1,2048]{2,0,1:T(8,128)(2,1)} %param.18), channel_id=1, source_target_pairs={{0,1},{1,2},{2,3},{3,4},{4,5},{5,6},{6,7},{7,8},{8,9},{9,10},{10,1... | collective-permute-start | bytes 786440 | tf_op jit(solution)/shard_map/ppermute | solution.py:31
  11.8 1.0 copy-start.15
  14.9 19.0 %copy-start.16 = (bf16[27,64,64]{2,1,0:T(8,128)(2,1)S(1)}, bf16[27,64,64]{2,1,0:T(8,128)(2,1)}, u32[]{:S(2)}) copy-start(bf16[27,64,64]{2,1,0:T(8,128)(2,1)} %param.20) | copy-start | bytes 663556
  15.2 18.2 %collective-permute-start.3 = (bf16[64,1,2048]{2,0,1:T(8,128)(2,1)S(1)}, bf16[64,1,2048]{2,0,1:T(8,128)(2,1)S(1)}, u32[]{:S(2)}, u32[]{:S(2)}) collective-permute-start(bf16[64,1,2048]{2,0,1:T(8,128)(2,1)S(1)} %bitcast.576), channel_id=1, source_target_pairs={{1,0},{2,1},{3,2},{4,3},{5,4},{6,5},{7,6},{8,7},{9,8},{10,9},{11,1... | collective-permute-start | bytes 786440 | tf_op jit(solution)/shard_map/ppermute | solution.py:34
  16.5 16.9 %collective-permute-start.2 = (bf16[64,1,2048]{2,0,1:T(8,128)(2,1)S(1)}, bf16[64,1,2048]{2,0,1:T(8,128)(2,1)S(1)}, u32[]{:S(2)}, u32[]{:S(2)}) collective-permute-start(bf16[64,1,2048]{2,0,1:T(8,128)(2,1)S(1)} %bitcast.577), channel_id=1, source_target_pairs={{0,1},{1,2},{2,3},{3,4},{4,5},{5,6},{6,7},{7,8},{8,9},{9,10},{10,1... | collective-permute-start | bytes 786440 | tf_op jit(solution)/shard_map/ppermute | solution.py:31
  25.7 34.3 %collective-permute-start.9 = (bf16[4,64,128]{2,1,0:T(8,128)(2,1)S(1)}, bf16[4,64,128]{2,1,0:T(8,128)(2,1)S(1)}, u32[]{:S(2)}, u32[]{:S(2)}) collective-permute-start(bf16[4,64,128]{2,1,0:T(8,128)(2,1)S(1)} %get-tuple-element.81), channel_id=1, source_target_pairs={{0,8},{1,9},{2,10},{3,11},{4,12},{5,13},{6,14},{7,15},{16,24},{17,... | collective-permute-start | bytes 196616 | tf_op jit(solution)/shard_map/ppermute | solution.py:52
  31.4 28.6 %collective-permute-start.10 = (bf16[4,64,128]{2,1,0:T(8,128)(2,1)S(1)}, bf16[4,64,128]{2,1,0:T(8,128)(2,1)S(1)}, u32[]{:S(2)}, u32[]{:S(2)}) collective-permute-start(bf16[4,64,128]{2,1,0:T(8,128)(2,1)S(1)} %get-tuple-element.82), channel_id=1, source_target_pairs={{8,0},{9,1},{10,2},{11,3},{12,4},{13,5},{14,6},{15,7},{24,16},{25,... | collective-permute-start | bytes 196616 | tf_op jit(solution)/shard_map/ppermute | solution.py:52
  40.4 0.9 copy-start.19
  40.7 5.9 %copy-start.18 = (s32[8,3]{0,1:T(4,128)S(1)}, s32[8,3]{0,1:T(4,128)}, u32[]{:S(2)}) copy-start(s32[8,3]{0,1:T(4,128)} %param.26) | copy-start | bytes 292
  40.7 16.0 %copy-start.21 = (s32[3]{0:T(128)S(1)}, s32[3]{0:T(128)}, u32[]{:S(2)}) copy-start(s32[3]{0:T(128)} %constant.246.clone.1) | copy-start | bytes 40
  40.7 21.6 %copy-start.2 = (f32[1,16,64,128]{3,2,1,0:T(8,128)S(1)}, f32[1,16,64,128]{3,2,1,0:T(8,128)}, u32[]{:S(2)}) copy-start(f32[1,16,64,128]{3,2,1,0:T(8,128)} %param.23) | copy-start | bytes 1572868
  41.6 5.0 %collective-permute-start.5 = (bf16[1,2048]{1,0:T(2,128)(2,1)S(1)}, bf16[1,2048]{1,0:T(2,128)(2,1)S(1)}, u32[]{:S(2)}, u32[]{:S(2)}) collective-permute-start(bf16[1,2048]{1,0:T(2,128)(2,1)S(1)} %convert_element_type.266), channel_id=1, source_target_pairs={{1,0},{2,1},{3,2},{4,3},{5,4},{6,5},{7,6},{8,7},{9,8},{10,9},{11,1... | collective-permute-start | bytes 12296 | tf_op jit(solution)/shard_map/ppermute | solution.py:34
  42.9 4.3 %collective-permute-start.4 = (bf16[1,2048]{1,0:T(2,128)(2,1)S(1)}, bf16[1,2048]{1,0:T(2,128)(2,1)S(1)}, u32[]{:S(2)}, u32[]{:S(2)}) collective-permute-start(bf16[1,2048]{1,0:T(2,128)(2,1)S(1)} %convert_element_type.266), channel_id=1, source_target_pairs={{0,1},{1,2},{2,3},{3,4},{4,5},{5,6},{6,7},{7,8},{8,9},{9,10},{10,1... | collective-permute-start | bytes 12296 | tf_op jit(solution)/shard_map/ppermute | solution.py:31
  47.4 6.8 %collective-permute-start.6 = (f32[1,2,2048]{2,1,0:T(2,128)S(1)}, f32[1,2,2048]{2,1,0:T(2,128)S(1)}, u32[]{:S(2)}, u32[]{:S(2)}) collective-permute-start(f32[1,2,2048]{2,1,0:T(2,128)S(1)} %pad_maximum_fusion.12), channel_id=1, source_target_pairs={{0,1},{1,0},{2,3},{3,2},{4,5},{5,4},{6,7},{7,6},{8,9},{9,8},{10,11... | collective-permute-start | bytes 49160 | tf_op jit(solution)/shard_map/ppermute | solution.py:42
  54.2 5.8 %collective-permute-start.7 = (f32[2,2,2048]{2,1,0:T(2,128)S(1)}, f32[2,2,2048]{2,1,0:T(2,128)S(1)}, u32[]{:S(2)}, u32[]{:S(2)}) collective-permute-start(f32[2,2,2048]{2,1,0:T(2,128)S(1)} %maximum_select_fusion.2), channel_id=1, source_target_pairs={{0,2},{1,3},{2,0},{3,1},{4,6},{5,7},{6,4},{7,5},{8,10},{9,11},{10,... | collective-permute-start | bytes 98312 | tf_op jit(solution)/shard_map/ppermute | solution.py:42
  60.1 5.2 %copy-start.11 = (f32[4,64,128]{2,1,0:T(8,128)}, f32[4,64,128]{2,1,0:T(8,128)S(1)}, u32[]{:S(2)}) copy-start(f32[4,64,128]{2,1,0:T(8,128)S(1)} %convert_element_type.271) | copy-start | bytes 393220
  60.1 4.5 %collective-permute-start.8 = (f32[4,2,2048]{2,1,0:T(2,128)S(1)}, f32[4,2,2048]{2,1,0:T(2,128)S(1)}, u32[]{:S(2)}, u32[]{:S(2)}) collective-permute-start(f32[4,2,2048]{2,1,0:T(2,128)S(1)} %maximum_select_fusion.1), channel_id=1, source_target_pairs={{0,4},{1,5},{2,6},{3,7},{4,0},{5,1},{6,2},{7,3},{8,12},{9,13},{10,... | collective-permute-start | bytes 196616 | tf_op jit(solution)/shard_map/ppermute | solution.py:42
  78.6 4.4 %copy-start.3 = (f32[16,64,128]{2,1,0:T(8,128)}, f32[16,64,128]{2,1,0:T(8,128)S(1)}, u32[]{:S(2)}) copy-start(f32[16,64,128]{2,1,0:T(8,128)S(1)} %copy.59) | copy-start | bytes 1572868
  85.8 7.1 %collective-permute-start.11 = (bf16[4,64,128]{2,1,0:T(8,128)(2,1)S(1)}, bf16[4,64,128]{2,1,0:T(8,128)(2,1)S(1)}, u32[]{:S(2)}, u32[]{:S(2)}) collective-permute-start(bf16[4,64,128]{2,1,0:T(8,128)(2,1)S(1)} %get-tuple-element.79), channel_id=1, source_target_pairs={{0,8},{1,9},{2,10},{3,11},{4,12},{5,13},{6,14},{7,15},{16,24},{17,... | collective-permute-start | bytes 196616 | tf_op jit(solution)/shard_map/ppermute | solution.py:52
  91.0 7.1 %collective-permute-start.12 = (bf16[4,64,128]{2,1,0:T(8,128)(2,1)S(1)}, bf16[4,64,128]{2,1,0:T(8,128)(2,1)S(1)}, u32[]{:S(2)}, u32[]{:S(2)}) collective-permute-start(bf16[4,64,128]{2,1,0:T(8,128)(2,1)S(1)} %get-tuple-element.80), channel_id=1, source_target_pairs={{8,0},{9,1},{10,2},{11,3},{12,4},{13,5},{14,6},{15,7},{24,16},{25,... | collective-permute-start | bytes 196616 | tf_op jit(solution)/shard_map/ppermute | solution.py:52
  106.3 5.3 %collective-permute-start.13 = (bf16[4,64,128]{2,1,0:T(8,128)(2,1)S(1)}, bf16[4,64,128]{2,1,0:T(8,128)(2,1)S(1)}, u32[]{:S(2)}, u32[]{:S(2)}) collective-permute-start(bf16[4,64,128]{2,1,0:T(8,128)(2,1)S(1)} %get-tuple-element.77), channel_id=1, source_target_pairs={{0,8},{1,9},{2,10},{3,11},{4,12},{5,13},{6,14},{7,15},{16,24},{17,... | collective-permute-start | bytes 196616 | tf_op jit(solution)/shard_map/ppermute | solution.py:52
  107.9 7.1 %collective-permute-start.14 = (bf16[4,64,128]{2,1,0:T(8,128)(2,1)S(1)}, bf16[4,64,128]{2,1,0:T(8,128)(2,1)S(1)}, u32[]{:S(2)}, u32[]{:S(2)}) collective-permute-start(bf16[4,64,128]{2,1,0:T(8,128)(2,1)S(1)} %get-tuple-element.78), channel_id=1, source_target_pairs={{8,0},{9,1},{10,2},{11,3},{12,4},{13,5},{14,6},{15,7},{24,16},{25,... | collective-permute-start | bytes 196616 | tf_op jit(solution)/shard_map/ppermute | solution.py:52
  115.0 0.7 copy-start.12
  120.4 7.0 %copy-start.5 = (f32[16,64,64,2]{2,0,1,3:T(8,128)S(1)}, f32[16,64,64,2]{2,0,1,3:T(8,128)}, u32[]{:S(2)}) copy-start(f32[16,64,64,2]{2,0,1,3:T(8,128)} %get-tuple-element.63) | copy-start | bytes 1572868
  123.2 11.6 %collective-permute-start.15 = (bf16[4,64,128]{2,1,0:T(8,128)(2,1)S(1)}, bf16[4,64,128]{2,1,0:T(8,128)(2,1)S(1)}, u32[]{:S(2)}, u32[]{:S(2)}) collective-permute-start(bf16[4,64,128]{2,1,0:T(8,128)(2,1)S(1)} %get-tuple-element.75), channel_id=1, source_target_pairs={{0,8},{1,9},{2,10},{3,11},{4,12},{5,13},{6,14},{7,15},{16,24},{17,... | collective-permute-start | bytes 196616 | tf_op jit(solution)/shard_map/ppermute | solution.py:52
  125.4 9.4 %collective-permute-start.16 = (bf16[4,64,128]{2,1,0:T(8,128)(2,1)S(1)}, bf16[4,64,128]{2,1,0:T(8,128)(2,1)S(1)}, u32[]{:S(2)}, u32[]{:S(2)}) collective-permute-start(bf16[4,64,128]{2,1,0:T(8,128)(2,1)S(1)} %get-tuple-element.76), channel_id=1, source_target_pairs={{8,0},{9,1},{10,2},{11,3},{12,4},{13,5},{14,6},{15,7},{24,16},{25,... | collective-permute-start | bytes 196616 | tf_op jit(solution)/shard_map/ppermute | solution.py:52
  133.2 2.1 %copy-start.7 = (f32[16,64,128]{2,1,0:T(8,128)S(1)}, f32[16,64,128]{2,1,0:T(8,128)}, u32[]{:S(2)}) copy-start(f32[16,64,128]{2,1,0:T(8,128)} %get-tuple-element.60) | copy-start | bytes 1572868
  133.2 2.1 %copy-start.8 = (f32[16,64,128]{2,1,0:T(8,128)S(1)}, f32[16,64,128]{2,1,0:T(8,128)}, u32[]{:S(2)}) copy-start(f32[16,64,128]{2,1,0:T(8,128)} %get-tuple-element.58) | copy-start | bytes 1572868
  133.2 2.1 %copy-start.9 = (f32[16,64,128]{2,1,0:T(8,128)S(1)}, f32[16,64,128]{2,1,0:T(8,128)}, u32[]{:S(2)}) copy-start(f32[16,64,128]{2,1,0:T(8,128)} %get-tuple-element.56) | copy-start | bytes 1572868
  134.7 1.0 copy-start.10
  134.8 1.4 copy-start.14
  136.1 3.4 %copy-start.4 = (f32[16,64,128]{2,1,0:T(8,128)S(1)}, f32[16,64,128]{2,1,0:T(8,128)}, u32[]{:S(2)}) copy-start(f32[16,64,128]{2,1,0:T(8,128)} %copy-done.3) | copy-start | bytes 1572868
  142.4 3.1 %copy-start.6 = (f32[16,64,128]{2,1,0:T(8,128)}, f32[16,64,128]{2,1,0:T(8,128)S(1)}, u32[]{:S(2)}) copy-start(f32[16,64,128]{2,1,0:T(8,128)S(1)} %scatter-add.19) | copy-start | bytes 1572868
  146.3 0.7 copy-start.22
  147.3 0.7 copy-start.20
  147.6 26.7 %copy-start.1 = (f32[8,4]{0,1:T(4,128)S(1)}, f32[8,4]{0,1:T(4,128)}, u32[]{:S(2)}) copy-start(f32[8,4]{0,1:T(4,128)} %param.25) | copy-start | bytes 388
  148.7 6.9 %collective-permute-start.22 = (f32[1,2048]{1,0:T(1,128)S(1)}, f32[1,2048]{1,0:T(1,128)S(1)}, u32[]{:S(2)}, u32[]{:S(2)}) collective-permute-start(f32[1,2048]{1,0:T(1,128)S(1)} %get-tuple-element.91), channel_id=1, source_target_pairs={{0,8},{1,9},{2,10},{3,11},{4,12},{5,13},{6,14},{7,15},{16,24},{17,... | collective-permute-start | bytes 24584 | tf_op jit(solution)/shard_map/ppermute | solution.py:52
  154.1 6.4 %collective-permute-start.21 = (f32[1,2048]{1,0:T(1,128)S(1)}, f32[1,2048]{1,0:T(1,128)S(1)}, u32[]{:S(2)}, u32[]{:S(2)}) collective-permute-start(f32[1,2048]{1,0:T(1,128)S(1)} %get-tuple-element.92), channel_id=1, source_target_pairs={{8,0},{9,1},{10,2},{11,3},{12,4},{13,5},{14,6},{15,7},{24,16},{25,... | collective-permute-start | bytes 24584 | tf_op jit(solution)/shard_map/ppermute | solution.py:52
  155.5 5.1 %collective-permute-start.17 = (f32[8,4,128]{2,1,0:T(4,128)S(1)}, f32[8,4,128]{2,1,0:T(4,128)S(1)}, u32[]{:S(2)}, u32[]{:S(2)}) collective-permute-start(f32[8,4,128]{2,1,0:T(4,128)S(1)} %broadcast_select_fusion.9), channel_id=1, source_target_pairs={{0,1},{1,0},{2,3},{3,2},{4,5},{5,4},{6,7},{7,6},{8,9},{9,8},{10,11... | collective-permute-start | bytes 49160 | tf_op jit(solution)/shard_map/ppermute | solution.py:21
  160.7 3.9 %collective-permute-start.18 = (f32[8,4,128]{2,1,0:T(4,128)S(1)}, f32[8,4,128]{2,1,0:T(4,128)S(1)}, u32[]{:S(2)}, u32[]{:S(2)}) collective-permute-start(f32[8,4,128]{2,1,0:T(4,128)S(1)} %fusion.474), channel_id=1, source_target_pairs={{0,2},{1,3},{2,0},{3,1},{4,6},{5,7},{6,4},{7,5},{8,10},{9,11},{10,... | collective-permute-start | bytes 49160 | tf_op jit(solution)/shard_map/ppermute | solution.py:21
  162.5 4.1 %collective-permute-start.23 = (f32[4,1,2048]{2,0,1:T(4,128)S(1)}, f32[4,1,2048]{2,0,1:T(4,128)S(1)}, u32[]{:S(2)}, u32[]{:S(2)}) collective-permute-start(f32[4,1,2048]{2,0,1:T(4,128)S(1)} %select_bitcast_fusion), channel_id=1, source_target_pairs={{0,4},{1,5},{2,6},{3,7},{4,0},{5,1},{6,2},{7,3},{8,12},{9,13},{10,... | collective-permute-start | bytes 98312 | tf_op jit(solution)/shard_map/ppermute | solution.py:42
  164.7 3.8 %collective-permute-start.19 = (f32[8,4,128]{2,1,0:T(4,128)S(1)}, f32[8,4,128]{2,1,0:T(4,128)S(1)}, u32[]{:S(2)}, u32[]{:S(2)}) collective-permute-start(f32[8,4,128]{2,1,0:T(4,128)S(1)} %fusion.500), channel_id=1, source_target_pairs={{0,4},{1,5},{2,6},{3,7},{4,0},{5,1},{6,2},{7,3},{8,12},{9,13},{10,... | collective-permute-start | bytes 49160 | tf_op jit(solution)/shard_map/ppermute | solution.py:21
  166.7 3.8 %collective-permute-start.24 = (f32[2,1,2048]{2,0,1:T(2,128)S(1)}, f32[2,1,2048]{2,0,1:T(2,128)S(1)}, u32[]{:S(2)}, u32[]{:S(2)}) collective-permute-start(f32[2,1,2048]{2,0,1:T(2,128)S(1)} %broadcast_select_fusion.4), channel_id=1, source_target_pairs={{0,2},{1,3},{2,0},{3,1},{4,6},{5,7},{6,4},{7,5},{8,10},{9,11},{10,... | collective-permute-start | bytes 49160 | tf_op jit(solution)/shard_map/ppermute | solution.py:42
  168.5 4.6 %collective-permute-start.20 = (f32[8,4,128]{2,1,0:T(4,128)S(1)}, f32[8,4,128]{2,1,0:T(4,128)S(1)}, u32[]{:S(2)}, u32[]{:S(2)}) collective-permute-start(f32[8,4,128]{2,1,0:T(4,128)S(1)} %add.1218), channel_id=1, source_target_pairs={{0,8},{1,9},{2,10},{3,11},{4,12},{5,13},{6,14},{7,15},{8,0},{9,1},... | collective-permute-start | bytes 49160 | tf_op jit(solution)/shard_map/ppermute | solution.py:21
  170.5 3.2 %collective-permute-start.25 = (f32[1,1,2048]{2,0,1:T(1,128)S(1)}, f32[1,1,2048]{2,0,1:T(1,128)S(1)}, u32[]{:S(2)}, u32[]{:S(2)}) collective-permute-start(f32[1,1,2048]{2,0,1:T(1,128)S(1)} %broadcast_select_fusion.5), channel_id=1, source_target_pairs={{0,1},{1,0},{2,3},{3,2},{4,5},{5,4},{6,7},{7,6},{8,9},{9,8},{10,11... | collective-permute-start | bytes 24584 | tf_op jit(solution)/shard_map/ppermute | solution.py:42
  (1 other events, 0.6 us)
